TPU v7x, 32 devices: a whole 2x2x4 slice. The times are simulated.
32 devices in a mesh: groups: 2 (over y), gx: 4 (over z), gy: 2 (over x), gz: 2 (over core).
Axes of the slice: x: 2, y: 2, z: 4, core: 2. Of those that a mesh axis runs over, the one named last changes fastest.
Arguments:
- coarse_state: float32 [8, 128, 32, 256], P(None, ('groups', 'gx'), 'gy', 'gz'), parts along dimension 1, may hold values from -6 to 6
- coarse_previous: float32 [8, 128, 32, 256], P(None, ('groups', 'gx'), 'gy', 'gz'), parts along dimension 1, may hold values from -6 to 6
- coarse_coefficient: float32 [2, 64, 32, 256], P(None, 'gx', 'gy', 'gz'), may hold values from 0.5 to 4
- fine_state: float32 [8, 128, 32, 256], P(None, ('groups', 'gx'), 'gy', 'gz'), parts along dimension 1, may hold values from -6 to 6
- fine_previous: float32 [8, 128, 32, 256], P(None, ('groups', 'gx'), 'gy', 'gz'), parts along dimension 1, may hold values from -6 to 6
- fine_coefficient: float32 [2, 64, 32, 256], P(None, 'gx', 'gy', 'gz'), may hold values from 0.5 to 4
- fine_parent: int32 [4, 2, 2, 2], P('gx', 'gy', 'gz'), may hold values from 0 to 3, as said below
- patch_dest: int32 [4, 2, 2, 2], P('gx', 'gy', 'gz'), may hold values from -1 to 3, as said below
Outputs:
- coarse_slope: float32 [8, 128, 32, 256], P(None, ('groups', 'gx'), 'gy', 'gz'), parts along dimension 1
- fine_slope: float32 [8, 128, 32, 256], P(None, ('groups', 'gx'), 'gy', 'gz'), parts along dimension 1
There are 2 independent parts, one for each index of `groups`. A program takes and returns all parts, laid end to end along the dimension named above; an argument that names none is the same for every part. Nothing has to cross between parts.
Inputs may be any that keep to these rules, and one draw needn't show every extreme that they name: fine_parent[i, j, k] = (g, c): the fine box at (i, j, k) refines candidate patch c of brick (g, j, k); no two fine boxes refine the same patch; c is 0 or 1. patch_dest[g, j, k, c] = i exactly when fine_parent[i, j, k] = (g, c), else -1.
All inputs are finite; a program needn't handle non-finite values.
Results may differ from a plain program's by a relative error of at most 0.0003.
Values sent between devices are 32-bit elements; how exact they have to be, the bound alone decides.
A program may use at most 64 MiB of HBM per device.

v0:
```python
import jax
import jax.numpy as jnp
from jax import lax
from jax.sharding import PartitionSpec as P

section_weight = 0.1


def padded_2(cells, sides, width):
    for axis, dim in sides:
        count = lax.axis_size(axis)
        ends = count - 1
        head = lax.slice_in_dim(cells, 0, width, axis=dim)
        tail = lax.slice_in_dim(cells, cells.shape[dim] - width, cells.shape[dim], axis=dim)
        cells = jnp.concatenate(
            [
                lax.ppermute(tail, axis, [(i, (i + 1) % count) for i in range(ends)]),
                cells,
                lax.ppermute(head, axis, [((i + 1) % count, i) for i in range(ends)]),
            ],
            axis=dim,
        )
    return cells


def operands(state, previous, coefficient):
    section_state = state + section_weight * previous
    modulus = coefficient[0]
    buoyancy = coefficient[1]
    return jnp.stack(
        [
            section_state[0],
            section_state[1],
            section_state[2],
            section_state[3],
            modulus * section_state[4],
            buoyancy * section_state[5],
            buoyancy * section_state[6],
            buoyancy * section_state[7],
        ]
    )


def select_fields(fields, direction):
    return jnp.stack([fields[0], fields[1 + direction], fields[4], fields[5 + direction]])


def derivative(extended, axis_number, spacing):
    interior = extended.shape[axis_number] - 4

    def offset(initial):
        return lax.slice_in_dim(extended, initial, initial + interior, axis=axis_number)

    return (offset(0) - 8.0 * offset(1) + 8.0 * offset(3) - offset(4)) / (12.0 * spacing)


def slopes(extended, coefficient, spacing):
    derived = [derivative(extended[direction], direction + 1, spacing) for direction in range(3)]
    modulus = coefficient[0]
    buoyancy = coefficient[1]
    pressure_rate = -modulus * (derived[0][1] + derived[1][1] + derived[2][1])
    adjoint_rate = -(derived[0][3] + derived[1][3] + derived[2][3])
    return jnp.stack(
        [
            pressure_rate,
            -buoyancy * derived[0][0],
            -buoyancy * derived[1][0],
            -buoyancy * derived[2][0],
            adjoint_rate,
            -derived[0][2],
            -derived[1][2],
            -derived[2][2],
        ]
    )


def upsample(face):
    return jnp.repeat(jnp.repeat(face, 2, axis=1), 2, axis=2)


def ghost_layers(face, direction):
    layered = jnp.expand_dims(upsample(face), direction + 1)
    shape_list = list(layered.shape)
    shape_list[direction + 1] = 2
    return jnp.broadcast_to(layered, tuple(shape_list))


def fine_extended(operand, lower_faces, upper_faces):
    return [
        jnp.concatenate(
            [
                ghost_layers(lower_faces[direction], direction),
                select_fields(operand, direction),
                ghost_layers(upper_faces[direction], direction),
            ],
            axis=direction + 1,
        )
        for direction in range(3)
    ]


def coarse_extended(padded):
    return [
        select_fields(padded, 0)[:, :, 2:-2, 2:-2],
        select_fields(padded, 1)[:, 2:-2, :, 2:-2],
        select_fields(padded, 2)[:, 2:-2, 2:-2, :],
    ]


def on_device(
    coarse_state,
    coarse_previous,
    coarse_coefficient,
    fine_state,
    fine_previous,
    fine_coefficient,
    fine_parent,
    patch_dest,
):
    coarse_operand = operands(coarse_state, coarse_previous, coarse_coefficient)
    padded = padded_2(coarse_operand, (("gx", 1), ("gy", 2), ("gz", 3)), 2)
    coarse_slope = slopes(coarse_extended(padded), coarse_coefficient, 1.0)
    halves = [extent // 2 for extent in coarse_state.shape[1:]]
    owners = lax.axis_size("gx")
    peer_rows = lax.iota(jnp.int32, owners)
    targets = patch_dest.reshape(2)
    parent = fine_parent.reshape(2)[0]
    routing = (peer_rows[:, None] == targets[None, :]).astype(jnp.float32)
    taking = (peer_rows == parent).astype(jnp.float32)
    anchors = [
        [candidate * halves[dimension] + 2 for dimension in range(3)] for candidate in range(2)
    ]
    pieces = []
    for candidate in range(2):
        anchor = anchors[candidate]
        window_piece = padded[
            :,
            anchor[0] - 1 : anchor[0] + halves[0] + 1,
            anchor[1] - 1 : anchor[1] + halves[1] + 1,
            anchor[2] - 1 : anchor[2] + halves[2] + 1,
        ]
        pieces.append(window_piece.reshape(8, -1))
    tail = (1,) * pieces[0].ndim
    incoming = lax.all_to_all(
        routing[:, 0].reshape((owners,) + tail) * pieces[0][None]
        + routing[:, 1].reshape((owners,) + tail) * pieces[1][None],
        "gx",
        split_axis=0,
        concat_axis=0,
        tiled=True,
    )
    rim_block = jnp.sum(
        taking.reshape((owners,) + (1,) * (incoming.ndim - 1)) * incoming, axis=0
    ).reshape(8, halves[0] + 2, halves[1] + 2, halves[2] + 2)
    lower_faces = [
        rim_block[:, 0, 1:-1, 1:-1],
        rim_block[:, 1:-1, 0, 1:-1],
        rim_block[:, 1:-1, 1:-1, 0],
    ]
    upper_faces = [
        rim_block[:, -1, 1:-1, 1:-1],
        rim_block[:, 1:-1, -1, 1:-1],
        rim_block[:, 1:-1, 1:-1, -1],
    ]
    lower_faces = [select_fields(lower_faces[direction], direction) for direction in range(3)]
    upper_faces = [select_fields(upper_faces[direction], direction) for direction in range(3)]
    fine_operand = operands(fine_state, fine_previous, fine_coefficient)
    fine_slope = slopes(
        fine_extended(fine_operand, lower_faces, upper_faces), fine_coefficient, 0.5
    )
    averaged = (
        fine_slope.reshape(8, halves[0], 2, halves[1], 2, halves[2], 2).sum(axis=(2, 4, 6)) * 0.125
    )
    returned = lax.all_to_all(
        taking.reshape(owners, 1, 1) * averaged.reshape(1, 8, -1),
        "gx",
        split_axis=0,
        concat_axis=0,
        tiled=True,
    )
    for candidate in range(2):
        picker = (peer_rows == targets[candidate]).astype(jnp.float32)
        averaged_patch = jnp.sum(picker.reshape(owners, 1, 1) * returned, axis=0).reshape(
            8, halves[0], halves[1], halves[2]
        )
        corner = [candidate * halves[dimension] for dimension in range(3)]
        window = (
            slice(None),
            slice(corner[0], corner[0] + halves[0]),
            slice(corner[1], corner[1] + halves[1]),
            slice(corner[2], corner[2] + halves[2]),
        )
        region = coarse_slope[window]
        coarse_slope = coarse_slope.at[window].set(
            jnp.where(targets[candidate] >= 0, averaged_patch, region)
        )
    return (coarse_slope, fine_slope)


def solution(mesh):
    in_specs = (
        P(None, ("groups", "gx"), "gy", "gz"),
        P(None, ("groups", "gx"), "gy", "gz"),
        P(None, "gx", "gy", "gz"),
        P(None, ("groups", "gx"), "gy", "gz"),
        P(None, ("groups", "gx"), "gy", "gz"),
        P(None, "gx", "gy", "gz"),
        P("gx", "gy", "gz", None),
        P("gx", "gy", "gz", None),
    )
    out_specs = (P(None, ("groups", "gx"), "gy", "gz"), P(None, ("groups", "gx"), "gy", "gz"))
    return jax.shard_map(
        on_device, mesh=mesh, in_specs=in_specs, out_specs=out_specs, check_vma=False
    )
```

profile of v0, /device:TPU:0, one launch (start us, length us, event | category | flops | bytes accessed | tf_op | source)
XLA Modules:
  0.0 264.5 jit_solution(2531852146360432269)
XLA Ops:
  2.6 5.1 %collective-permute-start = (f32[8,2,16,128]{3,2,1,0:T(8,128)S(1)}, f32[8,2,16,128]{3,2,1,0:T(8,128)S(1)}, u32[]{:S(2)}, u32[]{:S(2)}) collective-permute-start(f32[8,2,16,128]{3,2,1,0:T(8,128)S(1)} %get-tuple-element.69), channel_id=1, source_target_pairs={{0,4},{4,8},{8,12},{1,5},{5,9},{9,13},{2,6},{6,10},{10,14},{3,7},{... | collective-permute-start | bytes 393224 | tf_op jit(solution)/shard_map/ppermute | solution.py:17
  16.1 4.6 %collective-permute-start.2 = (f32[8,20,2,128]{3,0,2,1:T(8,128)S(1)}, f32[8,20,2,128]{3,0,2,1:T(8,128)S(1)}, u32[]{:S(2)}, u32[]{:S(2)}) collective-permute-start(f32[8,20,2,128]{3,0,2,1:T(8,128)S(1)} %copy.134), channel_id=1, source_target_pairs={{0,2},{1,3},{4,6},{5,7},{8,10},{9,11},{12,14},{13,15},{16,18},{17,... | collective-permute-start | bytes 491528 | tf_op jit(solution)/shard_map/ppermute | solution.py:17
  32.7 4.3 %collective-permute-start.4 = (f32[8,20,20,2]{2,0,3,1:T(8,128)}, f32[8,20,20,2]{2,0,3,1:T(8,128)}, u32[]{:S(2)}, u32[]{:S(2)}) collective-permute-start(f32[8,20,20,2]{2,0,3,1:T(8,128)} %copy.138), channel_id=1, source_target_pairs={{0,1},{2,3},{4,5},{6,7},{8,9},{10,11},{12,13},{14,15},{16,17},{18,... | collective-permute-start | bytes 76808 | tf_op jit(solution)/shard_map/ppermute | solution.py:17
  43.6 4.7 %pad_maximum_fusion = f32[8,20,20,132]{3,2,1,0:T(8,128)S(1)} fusion(f32[8,20,20,2]{3,2,1,0:T(8,128)} %copy.141, f32[8,20,2,128]{3,2,1,0:T(2,128)S(1)} %copy.137, f32[8,2,16,128]{3,2,1,0:T(8,128)} %copy-done.12, f32[8,16,16,128]{3,2,1,0:T(8,128)S(1)} %fusion.39, f32[8,2,16,128]{3,2,1,0:T(8,128)} %copy-done.10, f32[8,20,2,128]{3,2,1,0:T(2,128)} %copy-done.6, ...), kind=kLoop, calls=%fused_computation | loop fusion | flops 2534400 | bytes 3379200 | tf_op jit(solution)/shard_map/concatenate | solution.py:15
  58.3 3.9 %all-to-all-start = ((f32[4,8,6600]{2,1,0:T(8,128)}), f32[4,8,6600]{2,1,0:T(8,128)S(1)}, u32[]{:S(2)}, u32[]{:S(2)}) async-start(f32[4,8,6600]{2,1,0:T(8,128)} %multiply_add_fusion.2), calls=%async_computation | async-start | bytes 1703936 | tf_op jit(solution)/shard_map/all_to_all | solution.py:144
  69.4 14.3 %all-to-all-done = f32[4,8,6600]{2,1,0:T(8,128)S(1)} async-done(((f32[4,8,6600]{2,1,0:T(8,128)}), f32[4,8,6600]{2,1,0:T(8,128)S(1)}, u32[]{:S(2)}, u32[]{:S(2)}) %all-to-all-start) | async-done | bytes 844832 | tf_op jit(solution)/shard_map/all_to_all | solution.py:144
  91.6 9.8 %stack.112 = f32[1,8,2,8,2,64,2]{6,5,4,3,2,1,0:T(8,128)} reshape(f32[1,16,16,128]{3,2,1,0:T(8,128)S(1)} %get-tuple-element.88) | data formatting | bytes 262144 | tf_op jit(solution)/shard_map/stack | solution.py:63
  101.4 5.4 %copy.167 = f32[1,8,2,8,2,64,2]{5,3,6,4,2,1,0:T(8,128)S(1)} copy(f32[1,8,2,8,2,64,2]{6,5,4,3,2,1,0:T(8,128)} %stack.112) | data formatting | bytes 262144 | tf_op jit(solution)/shard_map/stack | solution.py:63
  106.8 9.8 %stack.111 = f32[1,8,2,8,2,64,2]{6,5,4,3,2,1,0:T(8,128)} reshape(f32[1,16,16,128]{3,2,1,0:T(8,128)S(1)} %get-tuple-element.90) | data formatting | bytes 262144 | tf_op jit(solution)/shard_map/stack | solution.py:63
  116.6 5.4 %copy.166 = f32[1,8,2,8,2,64,2]{5,3,6,4,2,1,0:T(8,128)S(1)} copy(f32[1,8,2,8,2,64,2]{6,5,4,3,2,1,0:T(8,128)} %stack.111) | data formatting | bytes 262144 | tf_op jit(solution)/shard_map/stack | solution.py:63
  122.0 9.8 %stack.110 = f32[1,8,2,8,2,64,2]{6,5,4,3,2,1,0:T(8,128)} reshape(f32[1,16,16,128]{3,2,1,0:T(8,128)S(1)} %get-tuple-element.92) | data formatting | bytes 262144 | tf_op jit(solution)/shard_map/stack | solution.py:63
  131.8 5.4 %copy.165 = f32[1,8,2,8,2,64,2]{5,3,6,4,2,1,0:T(8,128)S(1)} copy(f32[1,8,2,8,2,64,2]{6,5,4,3,2,1,0:T(8,128)} %stack.110) | data formatting | bytes 262144 | tf_op jit(solution)/shard_map/stack | solution.py:63
  137.2 9.8 %stack.109 = f32[1,8,2,8,2,64,2]{6,5,4,3,2,1,0:T(8,128)} reshape(f32[1,16,16,128]{3,2,1,0:T(8,128)S(1)} %get-tuple-element.39) | data formatting | bytes 262144 | tf_op jit(solution)/shard_map/stack | solution.py:63
  147.0 6.1 %copy.164 = f32[1,8,2,8,2,64,2]{5,3,6,4,2,1,0:T(8,128)} copy(f32[1,8,2,8,2,64,2]{6,5,4,3,2,1,0:T(8,128)} %stack.109) | data formatting | bytes 262144 | tf_op jit(solution)/shard_map/stack | solution.py:63
  153.1 9.8 %stack.108 = f32[1,8,2,8,2,64,2]{6,5,4,3,2,1,0:T(8,128)} reshape(f32[1,16,16,128]{3,2,1,0:T(8,128)S(1)} %copy-done.26) | data formatting | bytes 262144 | tf_op jit(solution)/shard_map/stack | solution.py:63
  162.9 6.1 %copy.163 = f32[1,8,2,8,2,64,2]{5,3,6,4,2,1,0:T(8,128)} copy(f32[1,8,2,8,2,64,2]{6,5,4,3,2,1,0:T(8,128)} %stack.108) | data formatting | bytes 262144 | tf_op jit(solution)/shard_map/stack | solution.py:63
  169.0 9.8 %stack.107 = f32[1,8,2,8,2,64,2]{6,5,4,3,2,1,0:T(8,128)} reshape(f32[1,16,16,128]{3,2,1,0:T(8,128)S(1)} %copy-done.25) | data formatting | bytes 262144 | tf_op jit(solution)/shard_map/stack | solution.py:63
  178.7 6.0 %copy.162 = f32[1,8,2,8,2,64,2]{5,3,6,4,2,1,0:T(8,128)} copy(f32[1,8,2,8,2,64,2]{6,5,4,3,2,1,0:T(8,128)} %stack.107) | data formatting | bytes 262144 | tf_op jit(solution)/shard_map/stack | solution.py:63
  184.8 9.8 %stack.106 = f32[1,8,2,8,2,64,2]{6,5,4,3,2,1,0:T(8,128)} reshape(f32[1,16,16,128]{3,2,1,0:T(8,128)S(1)} %get-tuple-element.45) | data formatting | bytes 262144 | tf_op jit(solution)/shard_map/stack | solution.py:63
  194.6 6.0 %copy.161 = f32[1,8,2,8,2,64,2]{5,3,6,4,2,1,0:T(8,128)} copy(f32[1,8,2,8,2,64,2]{6,5,4,3,2,1,0:T(8,128)} %stack.106) | data formatting | bytes 262144 | tf_op jit(solution)/shard_map/stack | solution.py:63
  200.6 9.8 %stack.105 = f32[1,8,2,8,2,64,2]{6,5,4,3,2,1,0:T(8,128)} reshape(f32[1,16,16,128]{3,2,1,0:T(8,128)S(1)} %get-tuple-element.47) | data formatting | bytes 262144 | tf_op jit(solution)/shard_map/stack | solution.py:63
  210.4 6.0 %copy.160 = f32[1,8,2,8,2,64,2]{5,3,6,4,2,1,0:T(8,128)} copy(f32[1,8,2,8,2,64,2]{6,5,4,3,2,1,0:T(8,128)} %stack.105) | data formatting | bytes 262144 | tf_op jit(solution)/shard_map/stack | solution.py:63
  228.0 11.3 %all-to-all-done.1 = f32[4,8,4096]{2,1,0:T(8,128)S(1)} async-done(((f32[4,8,4096]{2,1,0:T(8,128)}), f32[4,8,4096]{2,1,0:T(8,128)S(1)}, u32[]{:S(2)}, u32[]{:S(2)}) %all-to-all-start.1) | async-done | bytes 524320 | tf_op jit(solution)/shard_map/all_to_all | solution.py:174
  244.7 19.6 %scatter.9 = f32[8,16,16,128]{3,2,1,0:T(8,128)} dynamic-update-slice(f32[8,16,16,128]{3,2,1,0:T(8,128)} %scatter.6, f32[8,8,8,64]{3,2,1,0:T(8,128)S(1)} %slice_select_fusion, s32[]{:T(128)} %constant.79.clone.1, s32[]{:T(128)} %constant.83.clone.1, s32[]{:T(128)} %constant.83.clone.1, s32[]{:T(128)} %constant.84.clone.1) | dynamic-update-slice | bytes 262148 | tf_op jit(solution)/shard_map/scatter | solution.py:194
  (195 shorter events, 69.0 us)
Async XLA Ops:
  2.4 6.6 %copy-start.33 = (s32[1,1,1,2]{3,2,1,0:T(1,128)S(1)}, s32[1,1,1,2]{3,2,1,0:T(1,128)}, u32[]{:S(2)}) copy-start(s32[1,1,1,2]{3,2,1,0:T(1,128)} %param.19) | copy-start | bytes 28
  2.4 6.7 %copy-start.22 = (f32[8,16,16,128]{3,2,1,0:T(8,128)S(1)}, f32[8,16,16,128]{3,2,1,0:T(8,128)}, u32[]{:S(2)}) copy-start(f32[8,16,16,128]{3,2,1,0:T(8,128)} %param.15) | copy-start | bytes 3145732
  2.4 6.7 %copy-start.23 = (f32[8,16,16,128]{3,2,1,0:T(8,128)S(1)}, f32[8,16,16,128]{3,2,1,0:T(8,128)}, u32[]{:S(2)}) copy-start(f32[8,16,16,128]{3,2,1,0:T(8,128)} %param.16) | copy-start | bytes 3145732
  2.6 7.6 %copy-start.8 = (f32[2,16,16,128]{3,2,1,0:T(8,128)S(1)}, f32[2,16,16,128]{3,2,1,0:T(8,128)}, u32[]{:S(2)}) copy-start(f32[2,16,16,128]{3,2,1,0:T(8,128)} %param.17) | copy-start | bytes 786436
  2.6 8.6 %collective-permute-start = (f32[8,2,16,128]{3,2,1,0:T(8,128)S(1)}, f32[8,2,16,128]{3,2,1,0:T(8,128)S(1)}, u32[]{:S(2)}, u32[]{:S(2)}) collective-permute-start(f32[8,2,16,128]{3,2,1,0:T(8,128)S(1)} %get-tuple-element.69), channel_id=1, source_target_pairs={{0,4},{4,8},{8,12},{1,5},{5,9},{9,13},{2,6},{6,10},{10,14},{3,7},{... | collective-permute-start | bytes 393224 | tf_op jit(solution)/shard_map/ppermute | solution.py:17
  7.7 6.9 %collective-permute-start.1 = (f32[8,2,16,128]{3,2,1,0:T(8,128)S(1)}, f32[8,2,16,128]{3,2,1,0:T(8,128)S(1)}, u32[]{:S(2)}, u32[]{:S(2)}) collective-permute-start(f32[8,2,16,128]{3,2,1,0:T(8,128)S(1)} %get-tuple-element.70), channel_id=1, source_target_pairs={{4,0},{8,4},{12,8},{5,1},{9,5},{13,9},{6,2},{10,6},{14,10},{7,3},{... | collective-permute-start | bytes 393224 | tf_op jit(solution)/shard_map/ppermute | solution.py:19
  11.2 12.4 %copy-start.10 = (f32[8,2,16,128]{3,2,1,0:T(8,128)}, f32[8,2,16,128]{3,2,1,0:T(8,128)S(1)}, u32[]{:S(2)}) copy-start(f32[8,2,16,128]{3,2,1,0:T(8,128)S(1)} %collective-permute-done) | copy-start | bytes 393220
  14.6 9.0 %copy-start.12 = (f32[8,2,16,128]{3,2,1,0:T(8,128)}, f32[8,2,16,128]{3,2,1,0:T(8,128)S(1)}, u32[]{:S(2)}) copy-start(f32[8,2,16,128]{3,2,1,0:T(8,128)S(1)} %collective-permute-done.1) | copy-start | bytes 393220
  14.8 7.6 %collective-permute-start.3 = (f32[8,20,2,128]{3,0,2,1:T(8,128)S(1)}, f32[8,20,2,128]{3,0,2,1:T(8,128)S(1)}, u32[]{:S(2)}, u32[]{:S(2)}) collective-permute-start(f32[8,20,2,128]{3,0,2,1:T(8,128)S(1)} %copy.135), channel_id=1, source_target_pairs={{2,0},{3,1},{6,4},{7,5},{10,8},{11,9},{14,12},{15,13},{18,16},{19,... | collective-permute-start | bytes 491528 | tf_op jit(solution)/shard_map/ppermute | solution.py:19
  16.1 7.4 %collective-permute-start.2 = (f32[8,20,2,128]{3,0,2,1:T(8,128)S(1)}, f32[8,20,2,128]{3,0,2,1:T(8,128)S(1)}, u32[]{:S(2)}, u32[]{:S(2)}) collective-permute-start(f32[8,20,2,128]{3,0,2,1:T(8,128)S(1)} %copy.134), channel_id=1, source_target_pairs={{0,2},{1,3},{4,6},{5,7},{8,10},{9,11},{12,14},{13,15},{16,18},{17,... | collective-permute-start | bytes 491528 | tf_op jit(solution)/shard_map/ppermute | solution.py:17
  26.5 10.6 %copy-start.34 = (s32[1,1,1,2]{3,2,1,0:T(1,128)S(1)}, s32[1,1,1,2]{3,2,1,0:T(1,128)}, u32[]{:S(2)}) copy-start(s32[1,1,1,2]{3,2,1,0:T(1,128)} %param.18) | copy-start | bytes 28
  31.4 8.9 %collective-permute-start.5 = (f32[8,20,20,2]{2,0,3,1:T(8,128)}, f32[8,20,20,2]{2,0,3,1:T(8,128)}, u32[]{:S(2)}, u32[]{:S(2)}) collective-permute-start(f32[8,20,20,2]{2,0,3,1:T(8,128)} %copy.139), channel_id=1, source_target_pairs={{1,0},{3,2},{5,4},{7,6},{9,8},{11,10},{13,12},{15,14},{17,16},{19,... | collective-permute-start | bytes 76808 | tf_op jit(solution)/shard_map/ppermute | solution.py:19
  32.7 5.6 %collective-permute-start.4 = (f32[8,20,20,2]{2,0,3,1:T(8,128)}, f32[8,20,20,2]{2,0,3,1:T(8,128)}, u32[]{:S(2)}, u32[]{:S(2)}) collective-permute-start(f32[8,20,20,2]{2,0,3,1:T(8,128)} %copy.138), channel_id=1, source_target_pairs={{0,1},{2,3},{4,5},{6,7},{8,9},{10,11},{12,13},{14,15},{16,17},{18,... | collective-permute-start | bytes 76808 | tf_op jit(solution)/shard_map/ppermute | solution.py:17
  49.8 2.6 copy-start.13
  55.8 6.4 %copy-start.5 = (f32[2,20,20,132]{3,2,1,0:T(8,128)S(1)}, f32[2,20,20,132]{3,2,1,0:T(8,128)}, u32[]{:S(2)}) copy-start(f32[2,20,20,132]{3,2,1,0:T(8,128)} %get-tuple-element.49) | copy-start | bytes 1267204
  55.8 6.4 %copy-start.19 = (f32[1,20,20,132]{3,2,1,0:T(8,128)S(1)}, f32[1,20,20,132]{3,2,1,0:T(8,128)}, u32[]{:S(2)}) copy-start(f32[1,20,20,132]{3,2,1,0:T(8,128)} %get-tuple-element.51) | copy-start | bytes 633604
  55.8 6.4 %copy-start.20 = (f32[1,20,20,132]{3,2,1,0:T(8,128)S(1)}, f32[1,20,20,132]{3,2,1,0:T(8,128)}, u32[]{:S(2)}) copy-start(f32[1,20,20,132]{3,2,1,0:T(8,128)} %get-tuple-element.52) | copy-start | bytes 633604
  58.3 25.4 %all-to-all-start = ((f32[4,8,6600]{2,1,0:T(8,128)}), f32[4,8,6600]{2,1,0:T(8,128)S(1)}, u32[]{:S(2)}, u32[]{:S(2)}) async-start(f32[4,8,6600]{2,1,0:T(8,128)} %multiply_add_fusion.2), calls=%async_computation | async-start | bytes 1703936 | tf_op jit(solution)/shard_map/all_to_all | solution.py:144
  147.0 6.1 %copy-start.26 = (f32[1,16,16,128]{3,2,1,0:T(8,128)S(1)}, f32[1,16,16,128]{3,2,1,0:T(8,128)}, u32[]{:S(2)}) copy-start(f32[1,16,16,128]{3,2,1,0:T(8,128)} %get-tuple-element.41) | copy-start | bytes 393220
  162.9 6.1 %copy-start.25 = (f32[1,16,16,128]{3,2,1,0:T(8,128)S(1)}, f32[1,16,16,128]{3,2,1,0:T(8,128)}, u32[]{:S(2)}) copy-start(f32[1,16,16,128]{3,2,1,0:T(8,128)} %get-tuple-element.43) | copy-start | bytes 393220
  216.4 3.9 %copy-start.24 = (f32[1,8,2,8,2,64,2]{5,3,6,4,2,1,0:T(8,128)S(1)}, f32[1,8,2,8,2,64,2]{5,3,6,4,2,1,0:T(8,128)}, u32[]{:S(2)}) copy-start(f32[1,8,2,8,2,64,2]{5,3,6,4,2,1,0:T(8,128)} %copy.164) | copy-start | bytes 393220
  220.5 4.9 %copy-start.16 = (f32[4,16,16,128]{3,2,1,0:T(8,128)S(1)}, f32[4,16,16,128]{3,2,1,0:T(8,128)}, u32[]{:S(2)}) copy-start(f32[4,16,16,128]{3,2,1,0:T(8,128)} %copy-done.15) | copy-start | bytes 1572868
  220.8 4.5 %copy-start.18 = (f32[4,16,16,128]{3,2,1,0:T(8,128)S(1)}, f32[4,16,16,128]{3,2,1,0:T(8,128)}, u32[]{:S(2)}) copy-start(f32[4,16,16,128]{3,2,1,0:T(8,128)} %copy-done.17) | copy-start | bytes 1572868
  221.9 17.5 %all-to-all-start.1 = ((f32[4,8,4096]{2,1,0:T(8,128)}), f32[4,8,4096]{2,1,0:T(8,128)S(1)}, u32[]{:S(2)}, u32[]{:S(2)}) async-start(f32[4,8,4096]{2,1,0:T(8,128)} %broadcast_multiply_fusion), calls=%async_computation.1 | async-start | bytes 1048576 | tf_op jit(solution)/shard_map/all_to_all | solution.py:174
  (20 other events, 30.2 us)
where the time goes:
time: 266 us; the launch traced here: 264 us
  local copies, waits for them, and re-layouts  179 us (67%)
  waiting for transfers between devices  29.9 us (11%)
  other arithmetic  27.6 us (10%)
  starting transfers between devices  25.2 us (9%)
  between operations  2.95 us (1%)
    another operation x17, local copies, waits for them, and re-layouts, slopes(): jnp.stack([pressure_rate, -buoyancy * derived[0][0], -buoyancy * derived[...  125 us
    scatter x2, local copies, waits for them, and re-layouts, on_device(): coarse_slope.at[window]  22.5 us
    all_to_all x1, waiting for transfers between devices, on_device(): lax.all_to_all(routing[:, 0].reshape((owners,) + tail) * pieces[0][None]...  14.3 us
    ppermute x3, starting transfers between devices, padded_2(): lax.ppermute(tail, axis, [(i, (i + 1) % count) for i in range(ends)])  14 us
    all_to_all x1, waiting for transfers between devices, on_device(): lax.all_to_all(taking.reshape(owners, 1, 1) * averaged.reshape(1, 8, -1),...  11.3 us
    unnamed x78, local copies, waits for them, and re-layouts  9.43 us
    concatenate x3, other arithmetic, padded_2(): jnp.concatenate([lax.ppermute(tail, axis, [(i, (i + 1) % count) for i in...  6.97 us
    unnamed x17, other arithmetic  6.41 us
  transfers between devices with their start and end apart: 8, of which 4 were waited for; matrix products, arithmetic and copies ran while one was open for 5% of the time, Pallas kernels for 0%

commit v1 on v0

v1 whole, which is shorter than its diff:
```python
import functools

import jax
import jax.numpy as jnp
from jax import lax
from jax.experimental import pallas as pl
from jax.experimental.pallas import tpu as pltpu
from jax.sharding import PartitionSpec as P

section_weight = 0.1
MESH = pl.DeviceIdType.MESH
x_fields = (0, 1, 4, 5)
y_fields = (0, 2, 4, 6)
z_fields = (0, 3, 4, 7)


def split_dot(values, matrix):
    high = values.astype(jnp.bfloat16)
    low = (values - high.astype(jnp.float32)).astype(jnp.bfloat16)
    return jnp.dot(high, matrix, preferred_element_type=jnp.float32) + jnp.dot(
        low, matrix, preferred_element_type=jnp.float32
    )


def kernel(
    counts,
    parent_ref,
    dest_ref,
    cs_hbm,
    cp_hbm,
    cc_hbm,
    fs_hbm,
    fp_hbm,
    fc_hbm,
    co_hbm,
    fo_hbm,
    cs,
    cp,
    cc,
    fs,
    fp,
    fc,
    cop,
    fop,
    cez,
    fez,
    co,
    fo,
    ysend,
    yhalo,
    zsend,
    zhalo,
    rim_pair,
    rim_send,
    rim_recv,
    zup,
    xup,
    pairs,
    avg,
    in_sem,
    out_sem,
    hx_send,
    hx_recv,
    hy_send,
    hy_recv,
    hz_send,
    hz_recv,
    rim_ss,
    rim_rs,
    avg_ss,
    avg_rs,
):
    count_x, count_y, count_z = counts
    CX, CY, CZ = cs.shape[1:]
    PX, PY, PZ = CX // 2, CY // 2, CZ // 2
    me = lax.axis_index("gx")
    my = lax.axis_index("gy")
    mz = lax.axis_index("gz")
    loads = [
        pltpu.make_async_copy(source, target, in_sem.at[number])
        for number, (source, target) in enumerate(
            ((cs_hbm, cs), (cp_hbm, cp), (cc_hbm, cc), (fs_hbm, fs), (fp_hbm, fp), (fc_hbm, fc))
        )
    ]
    for load in loads:
        load.start()

    peers = [lax.rem(me + offset, count_x) for offset in range(count_x)]
    barrier = pltpu.get_barrier_semaphore()
    for offset in range(1, count_x):
        pl.semaphore_signal(barrier, inc=1, device_id={"gx": peers[offset]}, device_id_type=MESH)
    has = {
        ("gx", 0): me > 0,
        ("gx", 1): me < count_x - 1,
        ("gy", 0): my > 0,
        ("gy", 1): my < count_y - 1,
        ("gz", 0): mz > 0,
        ("gz", 1): mz < count_z - 1,
    }
    index = {"gx": me, "gy": my, "gz": mz}
    count = {"gx": count_x, "gy": count_y, "gz": count_z}

    def neighbour(axis, side):
        return {axis: lax.rem(index[axis] + (1 if side else count[axis] - 1), count[axis])}

    for axis in ("gy", "gz"):
        for side in range(2):

            @pl.when(has[axis, side])
            def _():
                pl.semaphore_signal(
                    barrier, inc=1, device_id=neighbour(axis, side), device_id_type=MESH
                )

    expected = count_x - 1
    for axis in ("gy", "gz"):
        for side in range(2):
            expected = expected + has[axis, side].astype(jnp.int32)

    lane = lax.broadcasted_iota(jnp.int32, (CY, CZ), 1)
    lane_half = lax.broadcasted_iota(jnp.int32, (PY, CZ), 1)
    inner = slice(8, 8 + CY)

    def operands(state, previous, coefficient, target):
        def step(x, carry):
            modulus = coefficient[0, x]
            buoyancy = coefficient[1, x]
            for field in range(8):
                value = state[field, x] + section_weight * previous[field, x]
                if field == 4:
                    value = modulus * value
                if field > 4:
                    value = buoyancy * value
                target[field, x + 2, inner, :] = value
            return carry

        lax.fori_loop(0, CX, step, 0)

    def slopes(op, ez, coefficient, out, scale):
        def step(x, carry):
            modulus = coefficient[0, x]
            buoyancy = coefficient[1, x]

            def dx(field):
                return scale * (
                    (op[field, x, inner, :] - op[field, x + 4, inner, :])
                    - 8.0 * (op[field, x + 1, inner, :] - op[field, x + 3, inner, :])
                )

            def dy(field):
                return scale * (
                    (op[field, x + 2, 6 : 6 + CY, :] - op[field, x + 2, 10 : 10 + CY, :])
                    - 8.0 * (op[field, x + 2, 7 : 7 + CY, :] - op[field, x + 2, 9 : 9 + CY, :])
                )

            def dz(number):
                own = op[z_fields[number], x + 2, inner, :]
                edge = ez[number, x]
                below = jnp.where(lane >= CZ - 2, edge, own)
                above = jnp.where(lane < 2, edge, own)
                below_1 = jnp.where(lane >= CZ - 1, edge, own)
                above_1 = jnp.where(lane < 1, edge, own)
                return scale * (
                    (pltpu.roll(below, 2, 1) - pltpu.roll(above, CZ - 2, 1))
                    - 8.0 * (pltpu.roll(below_1, 1, 1) - pltpu.roll(above_1, CZ - 1, 1))
                )

            out[0, x] = -modulus * (dx(1) + dy(2) + dz(1))
            out[1, x] = -buoyancy * dx(0)
            out[2, x] = -buoyancy * dy(0)
            out[3, x] = -buoyancy * dz(0)
            out[4, x] = -(dx(5) + dy(6) + dz(3))
            out[5, x] = -dx(4)
            out[6, x] = -dy(4)
            out[7, x] = -dz(2)
            return carry

        lax.fori_loop(0, CX, step, 0)

    for load in loads[:3]:
        load.wait()
    operands(cs, cp, cc, cop)

    for number, field in enumerate(y_fields):
        ysend[0, number] = cop[field, 2 : 2 + CX, 8:10, :]
        ysend[1, number] = cop[field, 2 : 2 + CX, 6 + CY : 8 + CY, :]
    for block in range(2):
        packed = jnp.zeros((CY, CZ), jnp.float32)
        for j in range(32):
            number, x = divmod(block * 32 + j, CX)
            shifted = pltpu.roll(cop[z_fields[number], x + 2, inner, :], (4 * j + 2) % CZ, 1)
            packed = jnp.where((lane >= 4 * j) & (lane < 4 * j + 4), shifted, packed)
        zsend[block] = packed

    pl.semaphore_wait(barrier, expected)

    def halo_copies(axis, side):
        if axis == "gx":
            first = 2 if side == 0 else CX
            land = 2 + CX if side == 0 else 0
            return [
                pltpu.make_async_remote_copy(
                    src_ref=cop.at[pl.ds(start, 2), pl.ds(first, 2), pl.ds(8, CY)],
                    dst_ref=cop.at[pl.ds(start, 2), pl.ds(land, 2), pl.ds(8, CY)],
                    send_sem=hx_send.at[side, half],
                    recv_sem=hx_recv.at[1 - side, half],
                    device_id=neighbour(axis, side),
                    device_id_type=MESH,
                )
                for half, start in enumerate((0, 4))
            ]
        if axis == "gy":
            return [
                pltpu.make_async_remote_copy(
                    src_ref=ysend.at[side],
                    dst_ref=yhalo.at[1 - side],
                    send_sem=hy_send.at[side],
                    recv_sem=hy_recv.at[1 - side],
                    device_id=neighbour(axis, side),
                    device_id_type=MESH,
                )
            ]
        return [
            pltpu.make_async_remote_copy(
                src_ref=zsend,
                dst_ref=zhalo.at[1 - side],
                send_sem=hz_send.at[side],
                recv_sem=hz_recv.at[1 - side],
                device_id=neighbour(axis, side),
                device_id_type=MESH,
            )
        ]

    halos = {key: halo_copies(*key) for key in has}
    for key in has:

        @pl.when(has[key])
        def _():
            for copy in halos[key]:
                copy.start()

    for side in range(2):

        @pl.when(jnp.logical_not(has["gx", side]))
        def _():
            land = 0 if side == 0 else 2 + CX
            for field in x_fields:
                cop[field, land : land + 2, inner, :] = jnp.zeros((2, CY, CZ), jnp.float32)

        @pl.when(jnp.logical_not(has["gy", side]))
        def _():
            yhalo[side] = jnp.zeros(yhalo.shape[1:], jnp.float32)

        @pl.when(jnp.logical_not(has["gz", side]))
        def _():
            zhalo[side] = jnp.zeros(zhalo.shape[1:], jnp.float32)

    for load in loads[3:]:
        load.wait()
    operands(fs, fp, fc, fop)

    for key in has:

        @pl.when(has[key])
        def _():
            for copy in halos[key[0], 1 - key[1]]:
                copy.wait_recv()

    for number, field in enumerate(y_fields):
        cop[field, 2 : 2 + CX, 6:8, :] = yhalo[0, number]
        cop[field, 2 : 2 + CX, 8 + CY : 10 + CY, :] = yhalo[1, number]
    for block in range(2):
        merged = jnp.where((lane & 3) < 2, zhalo[0, block], zhalo[1, block])
        for j in range(32):
            number, x = divmod(block * 32 + j, CX)
            cez[number, x] = pltpu.roll(merged, (CZ - 4 * j - 2) % CZ, 1)

    for base, fields in ((0, x_fields), (32, y_fields)):
        for pair in range(2):
            for side in range(2):
                row = base + (pair * 2 + side) * 8
                values = []
                for field in fields[2 * pair : 2 * pair + 2]:
                    for candidate in range(2):
                        if base == 0:
                            at = 2 + candidate * PX + (PX if side else -1)
                            y0 = 8 + candidate * PY
                            values.append(cop[field, at, y0 : y0 + PY, :])
                        else:
                            at = 8 + candidate * PY + (PY if side else -1)
                            x0 = 2 + candidate * PX
                            values.append(cop[field, x0 : x0 + PX, at, :])
                left = lane_half < PZ
                rim_pair[0, row : row + 8, :] = jnp.where(
                    left, values[0], pltpu.roll(values[2], PZ, 1)
                )
                rim_pair[1, row : row + 8, :] = jnp.where(
                    left, pltpu.roll(values[1], PZ, 1), values[3]
                )
    for candidate in range(2):
        packed = jnp.zeros((PY, CZ), jnp.float32)
        y0 = candidate * PY
        for number, field in enumerate(z_fields):
            for x in range(PX):
                i = number * PX + x
                own = cop[field, 2 + candidate * PX + x, 8 + y0 : 8 + y0 + PY, :]
                edge = cez[number, candidate * PX + x, y0 : y0 + PY, :]
                if candidate == 0:
                    lower = pltpu.roll(edge, (4 * i - (CZ - 1)) % CZ, 1)
                    upper = pltpu.roll(own, (4 * i + 2 - PZ) % CZ, 1)
                else:
                    lower = pltpu.roll(own, (4 * i - (PZ - 1)) % CZ, 1)
                    upper = pltpu.roll(edge, (4 * i + 2) % CZ, 1)
                packed = jnp.where(
                    lane_half == 4 * i, lower, jnp.where(lane_half == 4 * i + 2, upper, packed)
                )
        rim_pair[candidate, 64:72, :] = packed + pltpu.roll(packed, 1, 1)

    second = dest_ref[1]
    rims = []
    for offset in range(1, count_x):
        rim_send[offset] = jnp.where(second == peers[offset], rim_pair[1], rim_pair[0])
        rims.append(
            pltpu.make_async_remote_copy(
                src_ref=rim_send.at[offset],
                dst_ref=rim_recv.at[offset],
                send_sem=rim_ss.at[offset],
                recv_sem=rim_rs.at[offset],
                device_id={"gx": peers[offset]},
                device_id_type=MESH,
            )
        )
        rims[-1].start()
    rim_recv[0] = jnp.where(second == me, rim_pair[1], rim_pair[0])

    slopes(cop, cez, cc, co, 1.0 / 12.0)

    for rim in rims:
        rim.wait_recv()
    parent = parent_ref[0]
    rim_now = rim_recv[lax.rem(me - parent + count_x, count_x)]
    row_number = lax.broadcasted_iota(jnp.int32, (CZ, CZ), 0)
    column_number = lax.broadcasted_iota(jnp.int32, (CZ, CZ), 1)
    spread = [
        (row_number == (column_number >> 1) + half * PZ).astype(jnp.bfloat16) for half in range(2)
    ]
    gather = [
        jnp.where((row_number >> 1) + half * PZ == column_number, 0.125, 0.0).astype(jnp.bfloat16)
        for half in range(2)
    ]
    for half in range(2):
        wide = split_dot(rim_now[:64], spread[half])
        xup[half, 0, pl.ds(0, 64, 2), :] = wide
        xup[half, 0, pl.ds(1, 64, 2), :] = wide
    zup[pl.ds(0, PY, 2), :] = rim_now[64:72]
    zup[pl.ds(1, PY, 2), :] = rim_now[64:72]
    for pair in range(2):
        for half in range(2):
            for side in range(2):
                row = (pair * 2 + side) * 16
                face = xup[half, 0, row : row + 16, :]
                land = 2 + CX if side else 0
                fop[x_fields[2 * pair + half], land, inner, :] = face
                fop[x_fields[2 * pair + half], land + 1, inner, :] = face
                land = 8 + CY if side else 6
                for x in range(CX):
                    at = 64 + row + x
                    fop[y_fields[2 * pair + half], 2 + x, land : land + 2, :] = jnp.broadcast_to(
                        xup[half, 0, at : at + 1, :], (2, CZ)
                    )
    spread_z = zup[...]
    for number in range(4):
        for x in range(PX):
            i = number * PX + x
            edge = pltpu.roll(spread_z, (CZ - 4 * i - 2) % CZ, 1)
            fez[number, 2 * x] = edge
            fez[number, 2 * x + 1] = edge

    slopes(fop, fez, fc, fo, 1.0 / 6.0)
    fine_out = pltpu.make_async_copy(fo, fo_hbm, out_sem.at[0])
    fine_out.start()

    sums = []
    for field in range(8):
        folded = fo[field].reshape(PX, 2, CY, CZ)
        pairs[field] = (folded[:, 0] + folded[:, 1]).reshape(PX * CY, CZ)
        sums.append(
            pairs[field, pl.ds(0, PX * PY, 2), :] + pairs[field, pl.ds(1, PX * PY, 2), :]
        )
    for field in range(4):
        avg[0, field] = split_dot(sums[field], gather[0]) + split_dot(sums[field + 4], gather[1])
    sends = []
    for offset in range(1, count_x):
        sends.append(
            pltpu.make_async_remote_copy(
                src_ref=avg.at[0],
                dst_ref=avg.at[offset],
                send_sem=avg_ss.at[offset],
                recv_sem=avg_rs.at[offset],
                device_id={"gx": peers[offset]},
                device_id_type=MESH,
            )
        )
        sends[-1].start()

    for send in sends:
        send.wait_recv()

    lane_box = lax.broadcasted_iota(jnp.int32, (PX, PY, CZ), 2)
    for candidate in range(2):
        target = dest_ref[candidate]
        slot = lax.rem(me - jnp.maximum(target, 0) + count_x, count_x)
        here = (lane_box < PZ) if candidate == 0 else (lane_box >= PZ)
        keep = here & (jnp.full((PX, PY, CZ), target, jnp.int32) >= 0)
        xs = slice(candidate * PX, candidate * PX + PX)
        ys = slice(candidate * PY, candidate * PY + PY)
        for field in range(4):
            got = avg[slot, field]
            turned = pltpu.roll(got, PZ, 1)
            low, high = (got, turned) if candidate == 0 else (turned, got)
            for number, value in ((field, low), (field + 4, high)):
                co[number, xs, ys, :] = jnp.where(
                    keep, value.reshape(PX, PY, CZ), co[number, xs, ys, :]
                )
    coarse_out = pltpu.make_async_copy(co, co_hbm, out_sem.at[1])
    coarse_out.start()

    for key in has:

        @pl.when(has[key])
        def _():
            for copy in halos[key]:
                copy.wait_send()

    for copy in rims + sends:
        copy.wait_send()
    fine_out.wait()
    coarse_out.wait()


def on_device(counts, cs, cp, cc, fs, fp, fc, fine_parent, patch_dest):
    shape = cs.shape
    CX, CY, CZ = shape[1:]
    PX, PY = CX // 2, CY // 2
    count_x = counts[0]
    anywhere = pl.BlockSpec(memory_space=pl.ANY)
    scalar = pl.BlockSpec(memory_space=pltpu.SMEM)
    vmem = lambda *dims: pltpu.VMEM(dims, jnp.float32)
    dma = pltpu.SemaphoreType.DMA
    coarse, fine = pl.pallas_call(
        functools.partial(kernel, counts),
        out_shape=(
            jax.ShapeDtypeStruct(shape, jnp.float32),
            jax.ShapeDtypeStruct(shape, jnp.float32),
        ),
        in_specs=[scalar, scalar] + [anywhere] * 6,
        out_specs=(anywhere, anywhere),
        scratch_shapes=[
            vmem(*shape),
            vmem(*shape),
            vmem(*cc.shape),
            vmem(*shape),
            vmem(*shape),
            vmem(*cc.shape),
            vmem(8, CX + 4, CY + 16, CZ),
            vmem(8, CX + 4, CY + 16, CZ),
            vmem(4, CX, CY, CZ),
            vmem(4, CX, CY, CZ),
            vmem(*shape),
            vmem(*shape),
            vmem(2, 4, CX, 2, CZ),
            vmem(2, 4, CX, 2, CZ),
            vmem(2, CY, CZ),
            vmem(2, 2, CY, CZ),
            vmem(2, 72, CZ),
            vmem(count_x, 72, CZ),
            vmem(count_x, 72, CZ),
            vmem(CY, CZ),
            vmem(2, 1, 128, CZ),
            vmem(8, PX * CY, CZ),
            vmem(count_x, 4, PX * PY, CZ),
            dma((6,)),
            dma((2,)),
            dma((2, 2)),
            dma((2, 2)),
            dma((2,)),
            dma((2,)),
            dma((2,)),
            dma((2,)),
            dma((count_x,)),
            dma((count_x,)),
            dma((count_x,)),
            dma((count_x,)),
        ],
        compiler_params=pltpu.CompilerParams(
            collective_id=0, has_side_effects=True, vmem_limit_bytes=40 * 1024 * 1024
        ),
        cost_estimate=pl.CostEstimate(flops=8_000_000, bytes_accessed=6_800_000, transcendentals=0),
    )(fine_parent.reshape(2), patch_dest.reshape(2), cs, cp, cc, fs, fp, fc)
    return coarse, fine


def solution(mesh):
    counts = tuple(mesh.shape[axis] for axis in ("gx", "gy", "gz"))
    field_spec = P(None, ("groups", "gx"), "gy", "gz")
    coefficient_spec = P(None, "gx", "gy", "gz")
    index_spec = P("gx", "gy", "gz", None)
    return jax.shard_map(
        functools.partial(on_device, counts),
        mesh=mesh,
        in_specs=(
            field_spec,
            field_spec,
            coefficient_spec,
            field_spec,
            field_spec,
            coefficient_spec,
            index_spec,
            index_spec,
        ),
        out_specs=(field_spec, field_spec),
        check_vma=False,
    )
```

time: 266 us -> 37.6 us (0.14)
  local copies, waits for them, and re-layouts: 179 us -> 9.39 us
  waiting for transfers between devices: 29.9 us -> 0 us
  other arithmetic: 27.6 us -> 0 us
  Pallas kernels: 0 us -> 27.2 us
  starting transfers between devices: 25.2 us -> 0 us
    another operation x17 -> x0, local copies, waits for them, and re-layouts: 125 us -> none  [slopes(): jnp.stack([pressure_rate, -buoyancy * derived[0][0], -buoyancy * derived[...]
    pallas_call x0 -> x1, Pallas kernels: none -> 27.2 us  [on_device(): pl.pallas_call(functools.partial(kernel, counts), out_shape=(jax.ShapeDty...]
    all_to_all x2 -> x0, waiting for transfers between devices: 25.6 us -> none  [the longest x1 14.3 us: on_device(): lax.all_to_all(routing[:, 0].reshape((owners,) + tail) * pieces[0][None]...]
    scatter x2 -> x0, local copies, waits for them, and re-layouts: 22.5 us -> none  [on_device(): coarse_slope.at[window]]
    ppermute x6 -> x0, starting transfers between devices: 17.8 us -> none  [the longest x3 14 us: padded_2(): lax.ppermute(tail, axis, [(i, (i + 1) % count) for i in range(ends)])]
    slice x14 -> x0, local copies, waits for them, and re-layouts: 11.2 us -> none  [the longest x4 5.27 us: padded_2(): lax.slice_in_dim(cells, cells.shape[dim] - width, cells.shape[dim], axis=...]
    concatenate x6 -> x0, other arithmetic: 7.58 us -> none  [the longest x3 6.97 us: padded_2(): jnp.concatenate([lax.ppermute(tail, axis, [(i, (i + 1) % count) for i in...]
    all_to_all x2 -> x0, starting transfers between devices: 7.32 us -> none  [the longest x1 3.86 us: on_device(): lax.all_to_all(routing[:, 0].reshape((owners,) + tail) * pieces[0][None]...]
  transfers between devices with their start and end apart: 8 -> 0, of which waited for: 4 -> 0; matrix products, arithmetic and copies ran while one was open for 5% -> 0% of each run, Pallas kernels for 0% -> 0%
where the time goes in v1:
time: 37.6 us; the launch traced here: 37.3 us
  Pallas kernels  27.2 us (72%)
  local copies, waits for them, and re-layouts  9.39 us (25%)
  between operations  0.66 us (2%)
    pallas_call x1, Pallas kernels, on_device(): pl.pallas_call(functools.partial(kernel, counts), out_shape=(jax.ShapeDty...  27.2 us
    unnamed x18, local copies, waits for them, and re-layouts  9.39 us

profile of v1, /device:TPU:0, one launch (start us, length us, event | category | flops | bytes accessed | tf_op | source)
XLA Modules:
  0.0 37.3 jit_solution(3184300170341446687)
XLA Ops:
  0.6 0.0 copy-start.6
  0.6 0.0 copy-start.7
  0.7 0.6 %copy-done.6 = s32[1,1,1,2]{3,2,1,0:T(1,128)S(1)} copy-done((s32[1,1,1,2]{3,2,1,0:T(1,128)S(1)}, s32[1,1,1,2]{3,2,1,0:T(1,128)}, u32[]{:S(2)}) %copy-start.6) | copy-done | bytes 32
  1.3 0.0 copy-done.7
  1.3 0.0 copy-start
  1.3 1.2 %copy-done = f32[8,16,16,128]{3,2,1,0:T(8,128)S(1)} copy-done((f32[8,16,16,128]{3,2,1,0:T(8,128)S(1)}, f32[8,16,16,128]{3,2,1,0:T(8,128)}, u32[]{:S(2)}) %copy-start) | copy-done | bytes 1048600
  2.5 0.0 copy-start.1
  2.5 1.2 %copy-done.1 = f32[8,16,16,128]{3,2,1,0:T(8,128)S(1)} copy-done((f32[8,16,16,128]{3,2,1,0:T(8,128)S(1)}, f32[8,16,16,128]{3,2,1,0:T(8,128)}, u32[]{:S(2)}) %copy-start.1) | copy-done | bytes 1048600
  3.8 0.0 copy-start.2
  3.8 1.2 %copy-done.2 = f32[8,16,16,128]{3,2,1,0:T(8,128)S(1)} copy-done((f32[8,16,16,128]{3,2,1,0:T(8,128)S(1)}, f32[8,16,16,128]{3,2,1,0:T(8,128)}, u32[]{:S(2)}) %copy-start.2) | copy-done | bytes 1048600
  5.0 0.0 copy-start.3
  5.0 1.2 %copy-done.3 = f32[8,16,16,128]{3,2,1,0:T(8,128)S(1)} copy-done((f32[8,16,16,128]{3,2,1,0:T(8,128)S(1)}, f32[8,16,16,128]{3,2,1,0:T(8,128)}, u32[]{:S(2)}) %copy-start.3) | copy-done | bytes 1048600
  6.2 0.0 copy-start.4
  6.2 0.9 %copy-done.4 = f32[2,16,16,128]{3,2,1,0:T(8,128)S(1)} copy-done((f32[2,16,16,128]{3,2,1,0:T(8,128)S(1)}, f32[2,16,16,128]{3,2,1,0:T(8,128)}, u32[]{:S(2)}) %copy-start.4) | copy-done | bytes 262168
  7.2 0.0 copy-start.5
  7.2 0.9 %copy-done.5 = f32[2,16,16,128]{3,2,1,0:T(8,128)S(1)} copy-done((f32[2,16,16,128]{3,2,1,0:T(8,128)S(1)}, f32[2,16,16,128]{3,2,1,0:T(8,128)}, u32[]{:S(2)}) %copy-start.5) | copy-done | bytes 262168
  8.1 27.2 %shard_map.95 = (f32[8,16,16,128]{3,2,1,0:T(8,128)S(1)}, f32[8,16,16,128]{3,2,1,0:T(8,128)S(1)}) custom-call(s32[2]{0:T(128)S(1)} %bitcast.2, s32[2]{0:T(128)S(1)} %bitcast.3, f32[8,16,16,128]{3,2,1,0:T(8,128)S(1)} %copy-done, f32[8,16,16,128]{3,2,1,0:T(8,128)S(1)} %copy-done.1, f32[2,16,16,128]{3,2,1,0:T(8,128)S(1)} %copy-done.4, ...), custom_call_target="tpu_custom_call" | custom-call | flops 8000000 | bytes 6800000 | tf_op jit(solution)/shard_map/pallas_call | solution.py:450
  35.3 1.0 %copy.12 = f32[8,16,16,128]{3,2,1,0:T(8,128)} copy(f32[8,16,16,128]{3,2,1,0:T(8,128)S(1)} %get-tuple-element.4) | data formatting | bytes 2097152
  36.3 1.0 %copy.13 = f32[8,16,16,128]{3,2,1,0:T(8,128)} copy(f32[8,16,16,128]{3,2,1,0:T(8,128)S(1)} %get-tuple-element.5) | data formatting | bytes 2097152
Async XLA Ops:
  0.6 0.7 %copy-start.6 = (s32[1,1,1,2]{3,2,1,0:T(1,128)S(1)}, s32[1,1,1,2]{3,2,1,0:T(1,128)}, u32[]{:S(2)}) copy-start(s32[1,1,1,2]{3,2,1,0:T(1,128)} %param.14) | copy-start | bytes 28
  0.6 0.7 %copy-start.7 = (s32[1,1,1,2]{3,2,1,0:T(1,128)S(1)}, s32[1,1,1,2]{3,2,1,0:T(1,128)}, u32[]{:S(2)}) copy-start(s32[1,1,1,2]{3,2,1,0:T(1,128)} %param.15) | copy-start | bytes 28
  1.3 1.2 %copy-start = (f32[8,16,16,128]{3,2,1,0:T(8,128)S(1)}, f32[8,16,16,128]{3,2,1,0:T(8,128)}, u32[]{:S(2)}) copy-start(f32[8,16,16,128]{3,2,1,0:T(8,128)} %cs_hbm.1) | copy-start | bytes 3145732
  2.5 1.2 %copy-start.1 = (f32[8,16,16,128]{3,2,1,0:T(8,128)S(1)}, f32[8,16,16,128]{3,2,1,0:T(8,128)}, u32[]{:S(2)}) copy-start(f32[8,16,16,128]{3,2,1,0:T(8,128)} %cp_hbm.1) | copy-start | bytes 3145732
  3.8 1.2 %copy-start.2 = (f32[8,16,16,128]{3,2,1,0:T(8,128)S(1)}, f32[8,16,16,128]{3,2,1,0:T(8,128)}, u32[]{:S(2)}) copy-start(f32[8,16,16,128]{3,2,1,0:T(8,128)} %fs_hbm.1) | copy-start | bytes 3145732
  5.0 1.2 %copy-start.3 = (f32[8,16,16,128]{3,2,1,0:T(8,128)S(1)}, f32[8,16,16,128]{3,2,1,0:T(8,128)}, u32[]{:S(2)}) copy-start(f32[8,16,16,128]{3,2,1,0:T(8,128)} %fp_hbm.1) | copy-start | bytes 3145732
  6.2 0.9 %copy-start.4 = (f32[2,16,16,128]{3,2,1,0:T(8,128)S(1)}, f32[2,16,16,128]{3,2,1,0:T(8,128)}, u32[]{:S(2)}) copy-start(f32[2,16,16,128]{3,2,1,0:T(8,128)} %cc_hbm.1) | copy-start | bytes 786436
  7.2 0.9 %copy-start.5 = (f32[2,16,16,128]{3,2,1,0:T(8,128)S(1)}, f32[2,16,16,128]{3,2,1,0:T(8,128)}, u32[]{:S(2)}) copy-start(f32[2,16,16,128]{3,2,1,0:T(8,128)} %fc_hbm.1) | copy-start | bytes 786436

commit v2 on v1

--- a/solution.py
+++ b/solution.py
@@ -57,6 +57,7 @@
     xup,
     pairs,
     avg,
+    edges,
     in_sem,
     out_sem,
     hx_send,
@@ -259,6 +260,85 @@
         load.wait()
     operands(fs, fp, fc, fop)
 
+    for field in range(8):
+        for land in (0, 2 + CX):
+            fop[field, land : land + 2, inner, :] = jnp.zeros((2, CY, CZ), jnp.float32)
+    for field in y_fields:
+        for land in (6, 8 + CY):
+            fop[field, 2 : 2 + CX, land : land + 2, :] = jnp.zeros((CX, 2, CZ), jnp.float32)
+    fez[...] = jnp.zeros(fez.shape, jnp.float32)
+    slopes(fop, fez, fc, fo, 1.0 / 6.0)
+    row_number = lax.broadcasted_iota(jnp.int32, (CZ, CZ), 0)
+    column_number = lax.broadcasted_iota(jnp.int32, (CZ, CZ), 1)
+    spread = [
+        (row_number == (column_number >> 1) + half * PZ).astype(jnp.bfloat16) for half in range(2)
+    ]
+    gather = [
+        jnp.where((row_number >> 1) + half * PZ == column_number, 0.125, 0.0).astype(jnp.bfloat16)
+        for half in range(2)
+    ]
+
+    def quad_sums(number, values):
+        folded = values.reshape(PX, 2, CY, CZ)
+        pairs[number] = (folded[:, 0] + folded[:, 1]).reshape(PX * CY, CZ)
+        return pairs[number, pl.ds(0, PX * PY, 2), :] + pairs[number, pl.ds(1, PX * PY, 2), :]
+
+    sums = [quad_sums(field, fo[field]) for field in range(8)]
+    for field in range(4):
+        avg[0, field * 64 : field * 64 + 64, :] = split_dot(sums[field], gather[0]) + split_dot(
+            sums[field + 4], gather[1]
+        )
+    sixth = 1.0 / 6.0
+    edge_rows = []
+    for half, number in enumerate((1, 0)):
+        edges[half, 0:16, :] = sixth * (7.0 * fc[number, 0] - fc[number, 1])
+        edges[half, 16:32, :] = sixth * (fc[number, CX - 2] - 7.0 * fc[number, CX - 1])
+        edges[half, 32:48, :] = sixth * (7.0 * fc[number, :, 0, :] - fc[number, :, 1, :])
+        edges[half, 48:64, :] = sixth * (
+            fc[number, :, CY - 2, :] - 7.0 * fc[number, :, CY - 1, :]
+        )
+        edge_rows.append(
+            edges[half, pl.ds(0, 32, 2), :] + edges[half, pl.ds(1, 32, 2), :]
+        )
+    avg[0, 256:288, :] = split_dot(edge_rows[0], gather[0]) + split_dot(edge_rows[1], gather[1])
+    packed = jnp.where(
+        lane_half < 64, 0.0, jnp.where((lane_half & 3) == 0, 0.5, -0.5)
+    ) + jnp.zeros((PY, CZ), jnp.float32)
+    for half, number in enumerate((1, 0)):
+        whole = quad_sums(half, fc[number])
+        for x in range(PX):
+            i = half * PX + x
+            block = whole[x * PY : x * PY + PY]
+            lower = (0.125 * sixth) * (7.0 * block - pltpu.roll(block, CZ - 1, 1))
+            upper = (0.125 * sixth) * (pltpu.roll(block, 1, 1) - 7.0 * block)
+            packed = jnp.where(
+                lane_half == 4 * i,
+                pltpu.roll(lower, 4 * i, 1),
+                jnp.where(
+                    lane_half == 4 * i + 2,
+                    pltpu.roll(upper, (4 * i + 2 - (CZ - 1)) % CZ, 1),
+                    packed,
+                ),
+            )
+    avg[0, 288:296, :] = packed
+
+    sends = [
+        [
+            pltpu.make_async_remote_copy(
+                src_ref=avg.at[0, pl.ds(start, size)],
+                dst_ref=avg.at[offset, pl.ds(start, size)],
+                send_sem=avg_ss.at[offset, part],
+                recv_sem=avg_rs.at[offset, part],
+                device_id={"gx": peers[offset]},
+                device_id_type=MESH,
+            )
+            for offset in range(1, count_x)
+        ]
+        for part, (start, size) in enumerate(((0, 128), (128, 168)))
+    ]
+    for send in sends[0]:
+        send.start()
+
     for key in has:
 
         @pl.when(has[key])
@@ -333,21 +413,15 @@
         rims[-1].start()
     rim_recv[0] = jnp.where(second == me, rim_pair[1], rim_pair[0])
 
+    for send in sends[1]:
+        send.start()
+
     slopes(cop, cez, cc, co, 1.0 / 12.0)
 
     for rim in rims:
         rim.wait_recv()
     parent = parent_ref[0]
     rim_now = rim_recv[lax.rem(me - parent + count_x, count_x)]
-    row_number = lax.broadcasted_iota(jnp.int32, (CZ, CZ), 0)
-    column_number = lax.broadcasted_iota(jnp.int32, (CZ, CZ), 1)
-    spread = [
-        (row_number == (column_number >> 1) + half * PZ).astype(jnp.bfloat16) for half in range(2)
-    ]
-    gather = [
-        jnp.where((row_number >> 1) + half * PZ == column_number, 0.125, 0.0).astype(jnp.bfloat16)
-        for half in range(2)
-    ]
     for half in range(2):
         wide = split_dot(rim_now[:64], spread[half])
         xup[half, 0, pl.ds(0, 64, 2), :] = wide
@@ -380,30 +454,7 @@
     fine_out = pltpu.make_async_copy(fo, fo_hbm, out_sem.at[0])
     fine_out.start()
 
-    sums = []
-    for field in range(8):
-        folded = fo[field].reshape(PX, 2, CY, CZ)
-        pairs[field] = (folded[:, 0] + folded[:, 1]).reshape(PX * CY, CZ)
-        sums.append(
-            pairs[field, pl.ds(0, PX * PY, 2), :] + pairs[field, pl.ds(1, PX * PY, 2), :]
-        )
-    for field in range(4):
-        avg[0, field] = split_dot(sums[field], gather[0]) + split_dot(sums[field + 4], gather[1])
-    sends = []
-    for offset in range(1, count_x):
-        sends.append(
-            pltpu.make_async_remote_copy(
-                src_ref=avg.at[0],
-                dst_ref=avg.at[offset],
-                send_sem=avg_ss.at[offset],
-                recv_sem=avg_rs.at[offset],
-                device_id={"gx": peers[offset]},
-                device_id_type=MESH,
-            )
-        )
-        sends[-1].start()
-
-    for send in sends:
+    for send in sends[0] + sends[1]:
         send.wait_recv()
 
     lane_box = lax.broadcasted_iota(jnp.int32, (PX, PY, CZ), 2)
@@ -415,13 +466,52 @@
         xs = slice(candidate * PX, candidate * PX + PX)
         ys = slice(candidate * PY, candidate * PY + PY)
         for field in range(4):
-            got = avg[slot, field]
+            got = avg[slot, field * 64 : field * 64 + 64, :]
             turned = pltpu.roll(got, PZ, 1)
             low, high = (got, turned) if candidate == 0 else (turned, got)
             for number, value in ((field, low), (field + 4, high)):
                 co[number, xs, ys, :] = jnp.where(
                     keep, value.reshape(PX, PY, CZ), co[number, xs, ys, :]
                 )
+        weights = avg[slot, 256:296, :]
+        rim = rim_pair[candidate]
+        keep_face = keep[0]
+        zero = jnp.zeros((PY, CZ), jnp.float32)
+
+        def halves(row):
+            turned = pltpu.roll(row, PZ, 1)
+            return (row, turned) if candidate == 0 else (turned, row)
+
+        for side in range(2):
+            sign = -0.5 if side else 0.5
+            for base, outs in ((0, (1, 0, 5, 4)), (32, (2, 0, 6, 4))):
+                row = base + side * 8
+                scaled = weights[base // 2 + side * 8 : base // 2 + side * 8 + 8] * rim[
+                    row : row + 8
+                ]
+                plain = sign * rim[row + 16 : row + 24]
+                for number, value in zip(outs, halves(scaled) + halves(plain)):
+                    value = jnp.where(keep_face, value, zero)
+                    if base == 0:
+                        at = candidate * PX + side * (PX - 1)
+                        co[number, at, ys, :] += value
+                    else:
+                        at = candidate * PY + side * (PY - 1)
+                        co[number, xs, at, :] += value
+        shares = weights[32:40] * rim[64:72]
+        first = candidate * PZ
+        last = first + PZ - 1
+        for order, number in enumerate((3, 0, 7, 4)):
+            for x in range(PX):
+                i = order * PX + x
+                value = jnp.where(
+                    lane_half == first,
+                    pltpu.roll(shares, (first - 4 * i) % CZ, 1),
+                    jnp.where(
+                        lane_half == last, pltpu.roll(shares, (last - 4 * i - 2) % CZ, 1), zero
+                    ),
+                )
+                co[number, candidate * PX + x, ys, :] += jnp.where(keep_face, value, zero)
     coarse_out = pltpu.make_async_copy(co, co_hbm, out_sem.at[1])
     coarse_out.start()
 
@@ -432,7 +522,7 @@
             for copy in halos[key]:
                 copy.wait_send()
 
-    for copy in rims + sends:
+    for copy in rims + sends[0] + sends[1]:
         copy.wait_send()
     fine_out.wait()
     coarse_out.wait()
@@ -478,7 +568,8 @@
             vmem(CY, CZ),
             vmem(2, 1, 128, CZ),
             vmem(8, PX * CY, CZ),
-            vmem(count_x, 4, PX * PY, CZ),
+            vmem(count_x, 4 * PX * PY + 40, CZ),
+            vmem(2, 64, CZ),
             dma((6,)),
             dma((2,)),
             dma((2, 2)),
@@ -489,11 +580,11 @@
             dma((2,)),
             dma((count_x,)),
             dma((count_x,)),
-            dma((count_x,)),
-            dma((count_x,)),
+            dma((count_x, 2)),
+            dma((count_x, 2)),
         ],
         compiler_params=pltpu.CompilerParams(
-            collective_id=0, has_side_effects=True, vmem_limit_bytes=40 * 1024 * 1024
+            collective_id=0, has_side_effects=True, vmem_limit_bytes=60 * 1024 * 1024
         ),
         cost_estimate=pl.CostEstimate(flops=8_000_000, bytes_accessed=6_800_000, transcendentals=0),
     )(fine_parent.reshape(2), patch_dest.reshape(2), cs, cp, cc, fs, fp, fc)

time: 37.6 us -> 31.1 us (0.83)
  local copies, waits for them, and re-layouts: 9.39 us -> 3.33 us
    unnamed x18 -> x4, local copies, waits for them, and re-layouts: 9.39 us -> 3.33 us
where the time goes in v2:
time: 31.1 us; the launch traced here: 31 us
  Pallas kernels  27 us (87%)
  local copies, waits for them, and re-layouts  3.33 us (11%)
  between operations  0.65 us (2%)
    pallas_call x1, Pallas kernels, on_device(): pl.pallas_call(functools.partial(kernel, counts), out_shape=(jax.ShapeDty...  27 us
    unnamed x4, local copies, waits for them, and re-layouts  3.33 us

profile of v2, /device:TPU:0, one launch (start us, length us, event | category | flops | bytes accessed | tf_op | source)
XLA Modules:
  0.0 31.0 jit_solution(1121094650526200609)
XLA Ops:
  0.6 27.0 %shard_map.95 = (f32[8,16,16,128]{3,2,1,0:T(8,128)}, f32[8,16,16,128]{3,2,1,0:T(8,128)}) custom-call(s32[2]{0:T(128)} %bitcast.2, s32[2]{0:T(128)} %bitcast.3, f32[8,16,16,128]{3,2,1,0:T(8,128)} %cs_hbm.1, f32[8,16,16,128]{3,2,1,0:T(8,128)} %cp_hbm.1, f32[2,16,16,128]{3,2,1,0:T(8,128)} %cc_hbm.1, f32[8,16,16,128]{3,2,1,0:T(8,128)} %fs_hbm.1, ...), custom_call_target="tpu_custom_call" | custom-call | flops 8000000 | bytes 6800000 | tf_op jit(solution)/shard_map/pallas_call | solution.py:540
  27.6 0.0 copy-start
  27.6 2.4 %copy.12 = f32[8,16,16,128]{3,2,1,0:T(8,128)} copy(f32[8,16,16,128]{3,2,1,0:T(8,128)} %get-tuple-element.4) | data formatting | bytes 2097152
  30.0 0.0 copy-done
  30.0 1.0 %copy.13 = f32[8,16,16,128]{3,2,1,0:T(8,128)} copy(f32[8,16,16,128]{3,2,1,0:T(8,128)S(1)} %copy-done) | data formatting | bytes 2097152
Async XLA Ops:
  27.6 2.4 %copy-start = (f32[8,16,16,128]{3,2,1,0:T(8,128)S(1)}, f32[8,16,16,128]{3,2,1,0:T(8,128)}, u32[]{:S(2)}) copy-start(f32[8,16,16,128]{3,2,1,0:T(8,128)} %get-tuple-element.5) | copy-start | bytes 3145732

commit v3 on v2

--- a/solution.py
+++ b/solution.py
@@ -135,7 +135,7 @@
                 target[field, x + 2, inner, :] = value
             return carry
 
-        lax.fori_loop(0, CX, step, 0)
+        lax.fori_loop(0, CX, step, 0, unroll=4)
 
     def slopes(op, ez, coefficient, out, scale):
         def step(x, carry):
@@ -176,7 +176,7 @@
             out[7, x] = -dz(2)
             return carry
 
-        lax.fori_loop(0, CX, step, 0)
+        lax.fori_loop(0, CX, step, 0, unroll=4)
 
     for load in loads[:3]:
         load.wait()

time: 31.1 us -> 30.1 us (0.968)
  Pallas kernels: 27 us -> 26 us
    pallas_call x1, Pallas kernels: 27 us -> 26 us  [on_device(): pl.pallas_call(functools.partial(kernel, counts), out_shape=(jax.ShapeDty...]
where the time goes in v3:
time: 30.1 us; the launch traced here: 30 us
  Pallas kernels  26 us (86%)
  local copies, waits for them, and re-layouts  3.33 us (11%)
  between operations  0.65 us (2%)
    pallas_call x1, Pallas kernels, on_device(): pl.pallas_call(functools.partial(kernel, counts), out_shape=(jax.ShapeDty...  26 us
    unnamed x4, local copies, waits for them, and re-layouts  3.33 us

profile of v3, /device:TPU:0, one launch (start us, length us, event | category | flops | bytes accessed | tf_op | source)
XLA Modules:
  0.0 30.0 jit_solution(13611691109271042886)
XLA Ops:
  0.6 26.0 %shard_map.95 = (f32[8,16,16,128]{3,2,1,0:T(8,128)}, f32[8,16,16,128]{3,2,1,0:T(8,128)}) custom-call(s32[2]{0:T(128)} %bitcast.2, s32[2]{0:T(128)} %bitcast.3, f32[8,16,16,128]{3,2,1,0:T(8,128)} %cs_hbm.1, f32[8,16,16,128]{3,2,1,0:T(8,128)} %cp_hbm.1, f32[2,16,16,128]{3,2,1,0:T(8,128)} %cc_hbm.1, f32[8,16,16,128]{3,2,1,0:T(8,128)} %fs_hbm.1, ...), custom_call_target="tpu_custom_call" | custom-call | flops 8000000 | bytes 6800000 | tf_op jit(solution)/shard_map/pallas_call | solution.py:540
  26.6 0.0 copy-start
  26.7 2.4 %copy.12 = f32[8,16,16,128]{3,2,1,0:T(8,128)} copy(f32[8,16,16,128]{3,2,1,0:T(8,128)} %get-tuple-element.4) | data formatting | bytes 2097152
  29.0 0.0 copy-done
  29.0 1.0 %copy.13 = f32[8,16,16,128]{3,2,1,0:T(8,128)} copy(f32[8,16,16,128]{3,2,1,0:T(8,128)S(1)} %copy-done) | data formatting | bytes 2097152
Async XLA Ops:
  26.6 2.4 %copy-start = (f32[8,16,16,128]{3,2,1,0:T(8,128)S(1)}, f32[8,16,16,128]{3,2,1,0:T(8,128)}, u32[]{:S(2)}) copy-start(f32[8,16,16,128]{3,2,1,0:T(8,128)} %get-tuple-element.5) | copy-start | bytes 3145732
